TPU v7x, 32 devices: a whole 2x2x4 slice. The times are simulated.
32 devices in a mesh: dp: 8 (over y, x, core), tensor: 4 (over z).
Axes of the slice: x: 2, y: 2, z: 4, core: 2. Of those that a mesh axis runs over, the one named last changes fastest.
Arguments:
- inputs: bfloat16 [16, 256, 768], P('dp'), may hold values from -6 to 6
- condition: bfloat16 [16, 768], P('dp'), may hold values from -6 to 6
- cotangent: bfloat16 [16, 256, 768], P('dp'), may hold values from -6 to 6
- w_ada: float32 [6, 768, 768], P(None, 'tensor'), may hold values from -0.21875 to 0.21875
- w_qkv: float32 [3, 768, 768], P(None, 'tensor'), may hold values from -0.21875 to 0.21875
- w_proj: float32 [768, 768], P('tensor'), may hold values from -0.625 to 0.625
- w_up: float32 [4, 768, 768], P(None, 'tensor'), may hold values from -0.21875 to 0.21875
- w_down: float32 [4, 768, 768], P(None, 'tensor'), may hold values from -0.109375 to 0.109375
- biases: float32 [14, 768], P(None, 'tensor'), may hold values from -2.5 to 2.5
- momentum_ada: float32 [6, 768, 768], P(None, 'tensor'), as said below
- momentum_qkv: float32 [3, 768, 768], P(None, 'tensor'), as said below
- momentum_proj: float32 [768, 768], P('tensor'), as said below
- momentum_up: float32 [4, 768, 768], P(None, 'tensor'), as said below
- momentum_down: float32 [4, 768, 768], P(None, 'tensor'), as said below
- bias_first: float32 [14, 768], P(None, 'tensor'), as said below
- bias_second: float32 [14, 768], P(None, 'tensor'), as said below
Outputs:
- output: bfloat16 [16, 256, 768], P('dp')
- grad_inputs: bfloat16 [16, 256, 768], P('dp')
- grad_condition: float32 [16, 768], P('dp')
- new_w_ada: float32 [6, 768, 768], P(None, 'tensor', 'dp')
- new_w_qkv: float32 [3, 768, 768], P(None, 'tensor', 'dp')
- new_w_proj: float32 [768, 768], P('tensor', 'dp')
- new_w_up: float32 [4, 768, 768], P(None, 'tensor', 'dp')
- new_w_down: float32 [4, 768, 768], P(None, 'tensor', 'dp')
- new_momentum_ada: float32 [6, 768, 768], P(None, 'tensor')
- new_momentum_qkv: float32 [3, 768, 768], P(None, 'tensor')
- new_momentum_proj: float32 [768, 768], P('tensor')
- new_momentum_up: float32 [4, 768, 768], P(None, 'tensor')
- new_momentum_down: float32 [4, 768, 768], P(None, 'tensor')
- new_biases: float32 [14, 768], P(None, 'tensor')
- new_bias_first: float32 [14, 768], P(None, 'tensor')
- new_bias_second: float32 [14, 768], P(None, 'tensor')
Inputs may be any that keep to these rules, and one draw needn't show every extreme that they name: `momentum_ada`: float32 values of either sign. `momentum_qkv`: float32 values of either sign. `momentum_proj`: float32 values of either sign. `momentum_up`: float32 values of either sign. `momentum_down`: float32 values of either sign. `bias_first`: float32 values of either sign. `bias_second`: positive float32 values.
All inputs are finite; a program needn't handle non-finite values.
Results may differ from a plain program's by a relative error of at most 0.0203.
Values may be sent and summed in bfloat16 or wider, within the bound.
No kernel may reach another device: no remote copies, remote signals or barrier semaphores. Data moves between devices by JAX's collectives and lax.ppermute only.
A program may use at most 192 MiB of HBM per device.

v0:
```python
import math

import jax
import jax.numpy as jnp
from jax import lax
from jax.sharding import PartitionSpec as P

HEAD_DIM = 64
NS_ITERS = 5
STEP = 10


NS_A = 3.4445
NS_B = -4.775
NS_C = 2.0315
MUON_RATE = 0.16
MUON_DECAY = 0.01
MUON_MOMENTUM = 0.95
ADAM_RATE = 0.25
BETA_ONE = 0.9
BETA_TWO = 0.999
ADAM_EPS = 1e-08
NORM_EPS = 1e-06


def shortened(value):
    return jax.tree.map(lambda a: a.astype(jnp.bfloat16) if a.dtype == jnp.float32 else a, value)


def from_root(block, axis, holder):
    block = jnp.where(lax.axis_index(axis) == holder, block, jnp.zeros_like(block))
    return lax.psum(block, axis)


def layer_norm(values):
    average = jnp.mean(values, axis=-1, keepdims=True)
    centered = values - average
    variance = jnp.mean(centered * centered, axis=-1, keepdims=True)
    return centered * lax.rsqrt(variance + NORM_EPS)


def modulate(values, shift_by, scale_by):
    return layer_norm(values) * (1.0 + scale_by[:, None, :]) + shift_by[:, None, :]


def gelu_tanh(values):
    return jax.nn.gelu(values, approximate=True)


def orthogonalize(start):
    current = start
    for iteration in range(NS_ITERS):
        gram = jnp.einsum("in,jn->ij", current, current, preferred_element_type=jnp.float32).astype(
            jnp.bfloat16
        )
        square = jnp.dot(gram, gram, preferred_element_type=jnp.float32)
        poly = (NS_B * gram.astype(jnp.float32) + NS_C * square).astype(jnp.bfloat16)
        product = jnp.dot(poly, current, preferred_element_type=jnp.float32)
        current = (NS_A * current.astype(jnp.float32) + product).astype(jnp.bfloat16)
    return current


def orient(matrix, matrix_index):
    if matrix_index != 2:
        return matrix.reshape(-1, matrix.shape[-1]).T
    return matrix


def restore(matrix, matrix_index, whole_shape):
    if matrix_index != 2:
        return matrix.T.reshape(whole_shape)
    return matrix.reshape(whole_shape)


def make_branch(chosen):

    def branch(matrices):
        results = []
        for matrix_index in range(len(matrices)):
            if matrix_index == chosen:
                results.append(orthogonalize(matrices[matrix_index]))
            else:
                results.append(jnp.zeros_like(matrices[matrix_index]))
        return tuple(results)

    return branch


def on_device(
    inputs,
    condition,
    cotangent,
    w_ada,
    w_qkv,
    w_proj,
    w_up,
    w_down,
    biases,
    momentum_ada,
    momentum_qkv,
    momentum_proj,
    momentum_up,
    momentum_down,
    bias_first,
    bias_second,
):
    quarter = w_ada.shape[1]
    latent_count = inputs.shape[0]
    seq_length = inputs.shape[1]
    heads_here = quarter // HEAD_DIM
    offset = lax.axis_index("tensor") * quarter
    scale_factor = 1.0 / math.sqrt(HEAD_DIM)
    ada_low = w_ada.astype(jnp.bfloat16)
    qkv_low = w_qkv.astype(jnp.bfloat16)
    proj_low = w_proj.astype(jnp.bfloat16)
    up_low = w_up.astype(jnp.bfloat16)
    down_low = w_down.astype(jnp.bfloat16)
    cond_act, silu_pull = jax.vjp(jax.nn.silu, condition.astype(jnp.float32))
    cond_low = cond_act.astype(jnp.bfloat16)
    mod_part = (
        jnp.einsum("bd,ked->bke", cond_low, ada_low, preferred_element_type=jnp.float32)
        + biases[0:6]
    )
    out_bias_part = jnp.stack([biases[8], biases[13]])
    modulation, out_bias = (
        lax.all_gather(mod_part, "tensor", axis=2, tiled=True),
        lax.all_gather(out_bias_part, "tensor", axis=1, tiled=True),
    )
    inputs_f = inputs.astype(jnp.float32)
    hidden_first, first_pull = jax.vjp(modulate, inputs_f, modulation[:, 0], modulation[:, 1])
    first_low = hidden_first.astype(jnp.bfloat16)
    projected = jnp.einsum("bsd,ked->bske", first_low, qkv_low, preferred_element_type=jnp.float32)
    head_shape = (latent_count, seq_length, heads_here, HEAD_DIM)
    query_heads = (projected[:, :, 0] + biases[6]).astype(jnp.bfloat16).reshape(head_shape)
    key_heads = projected[:, :, 1].astype(jnp.bfloat16).reshape(head_shape)
    value_heads = (projected[:, :, 2] + biases[7]).astype(jnp.bfloat16).reshape(head_shape)
    scores = (
        jnp.einsum("bqhc,bkhc->bhqk", query_heads, key_heads, preferred_element_type=jnp.float32)
        * scale_factor
    )
    row_top = jnp.max(scores, axis=-1, keepdims=True)
    log_total = row_top + jnp.log(jnp.sum(jnp.exp(scores - row_top), axis=-1, keepdims=True))
    probs_low = jnp.exp(scores - log_total).astype(jnp.bfloat16)
    attended = jnp.einsum(
        "bhqk,bkhc->bqhc", probs_low, value_heads, preferred_element_type=jnp.float32
    )
    attended_low = attended.reshape(latent_count, seq_length, quarter).astype(jnp.bfloat16)
    partial_first = jnp.einsum(
        "bsd,de->bse", attended_low, proj_low, preferred_element_type=jnp.float32
    )
    branch_first = (
        lax.psum(partial_first.astype(jnp.bfloat16), "tensor").astype(jnp.float32) + out_bias[0]
    )
    gate_first = modulation[:, 2][:, None, :]
    middle = inputs_f + gate_first * branch_first
    hidden_second, second_pull = jax.vjp(modulate, middle, modulation[:, 3], modulation[:, 4])
    second_low = hidden_second.astype(jnp.bfloat16)
    pre_act = (
        jnp.einsum("bsd,red->bsre", second_low, up_low, preferred_element_type=jnp.float32)
        + biases[9:13]
    )
    activated, gelu_pull = jax.vjp(gelu_tanh, pre_act)
    act_low = activated.astype(jnp.bfloat16)
    partial_second = jnp.einsum(
        "bsre,red->bsd", act_low, down_low, preferred_element_type=jnp.float32
    )
    branch_second = (
        lax.psum(partial_second.astype(jnp.bfloat16), "tensor").astype(jnp.float32) + out_bias[1]
    )
    gate_second = modulation[:, 5][:, None, :]
    output = (middle + gate_second * branch_second).astype(jnp.bfloat16)
    tangent = cotangent.astype(jnp.float32)
    d_branch_second = gate_second * tangent
    d_gate_second = jnp.sum(tangent * branch_second, axis=1)
    d_down_bias = jnp.sum(d_branch_second, axis=(0, 1))
    d_second_low = d_branch_second.astype(jnp.bfloat16)
    grad_down = jnp.einsum(
        "bsre,bsd->red", act_low, d_second_low, preferred_element_type=jnp.float32
    )
    d_act = jnp.einsum("bsd,red->bsre", d_second_low, down_low, preferred_element_type=jnp.float32)
    d_pre = gelu_pull(d_act)[0]
    d_up_bias = jnp.sum(d_pre, axis=(0, 1))
    d_pre_low = d_pre.astype(jnp.bfloat16)
    grad_up = jnp.einsum("bsre,bsd->red", d_pre_low, second_low, preferred_element_type=jnp.float32)
    d_second_part = jnp.einsum(
        "bsre,red->bsd", d_pre_low, up_low, preferred_element_type=jnp.float32
    )
    d_hidden_second = lax.psum(d_second_part.astype(jnp.bfloat16), "tensor").astype(jnp.float32)
    d_middle_norm, d_shift_second, d_scale_second = second_pull(d_hidden_second)
    d_middle = tangent + d_middle_norm
    d_branch_first = gate_first * d_middle
    d_gate_first = jnp.sum(d_middle * branch_first, axis=1)
    d_proj_bias = jnp.sum(d_branch_first, axis=(0, 1))
    d_first_low = d_branch_first.astype(jnp.bfloat16)
    grad_proj = jnp.einsum(
        "bsd,bse->de", attended_low, d_first_low, preferred_element_type=jnp.float32
    )
    d_attended = jnp.einsum(
        "bse,de->bsd", d_first_low, proj_low, preferred_element_type=jnp.float32
    )
    d_attended = d_attended.astype(jnp.bfloat16).reshape(head_shape)
    scores_again = (
        jnp.einsum("bqhc,bkhc->bhqk", query_heads, key_heads, preferred_element_type=jnp.float32)
        * scale_factor
    )
    probs = jnp.exp(scores_again - log_total)
    probs_again = probs.astype(jnp.bfloat16)
    d_values = jnp.einsum(
        "bhqk,bqhc->bkhc", probs_again, d_attended, preferred_element_type=jnp.float32
    )
    d_probs = jnp.einsum(
        "bqhc,bkhc->bhqk", d_attended, value_heads, preferred_element_type=jnp.float32
    )
    d_scores = (probs * (d_probs - jnp.sum(probs * d_probs, axis=-1, keepdims=True))).astype(
        jnp.bfloat16
    )
    d_queries = (
        jnp.einsum("bhqk,bkhc->bqhc", d_scores, key_heads, preferred_element_type=jnp.float32)
        * scale_factor
    )
    d_keys = (
        jnp.einsum("bhqk,bqhc->bkhc", d_scores, query_heads, preferred_element_type=jnp.float32)
        * scale_factor
    )
    flat_shape = (latent_count, seq_length, quarter)
    d_projected = jnp.stack(
        [d_queries.reshape(flat_shape), d_keys.reshape(flat_shape), d_values.reshape(flat_shape)],
        axis=2,
    )
    d_query_bias = jnp.sum(d_projected[:, :, 0], axis=(0, 1))
    d_value_bias = jnp.sum(d_projected[:, :, 2], axis=(0, 1))
    d_projected_low = d_projected.astype(jnp.bfloat16)
    grad_qkv = jnp.einsum(
        "bske,bsd->ked", d_projected_low, first_low, preferred_element_type=jnp.float32
    )
    d_first_part = jnp.einsum(
        "bske,ked->bsd", d_projected_low, qkv_low, preferred_element_type=jnp.float32
    )
    d_hidden_first = lax.psum(d_first_part.astype(jnp.bfloat16), "tensor").astype(jnp.float32)
    d_inputs_norm, d_shift_first, d_scale_first = first_pull(d_hidden_first)
    grad_inputs = (d_middle + d_inputs_norm).astype(jnp.bfloat16)
    d_modulation = jnp.stack(
        [d_shift_first, d_scale_first, d_gate_first, d_shift_second, d_scale_second, d_gate_second],
        axis=1,
    )
    d_mod_own = lax.dynamic_slice_in_dim(d_modulation, offset, quarter, 2)
    d_ada_bias = jnp.sum(d_mod_own, axis=0)
    d_mod_low = d_mod_own.astype(jnp.bfloat16)
    grad_ada = jnp.einsum("bke,bd->ked", d_mod_low, cond_low, preferred_element_type=jnp.float32)
    d_cond_part = jnp.einsum("bke,ked->bd", d_mod_low, ada_low, preferred_element_type=jnp.float32)
    d_cond_act = lax.psum(d_cond_part, "tensor")
    grad_condition = silu_pull(d_cond_act)[0]
    d_proj_own = lax.dynamic_slice_in_dim(d_proj_bias, offset, quarter, 0)
    d_down_own = lax.dynamic_slice_in_dim(d_down_bias, offset, quarter, 0)
    grad_biases = jnp.concatenate(
        [
            d_ada_bias,
            d_query_bias[None],
            d_value_bias[None],
            d_proj_own[None],
            d_up_bias,
            d_down_own[None],
        ],
        axis=0,
    )
    grad_ada, grad_qkv, grad_proj, grad_up, grad_down, grad_biases = lax.psum(
        (grad_ada, grad_qkv, grad_proj, grad_up, grad_down, grad_biases), "dp"
    )
    moment_ada = MUON_MOMENTUM * momentum_ada + grad_ada
    moment_qkv = MUON_MOMENTUM * momentum_qkv + grad_qkv
    moment_proj = MUON_MOMENTUM * momentum_proj + grad_proj
    moment_up = MUON_MOMENTUM * momentum_up + grad_up
    moment_down = MUON_MOMENTUM * momentum_down + grad_down
    gather_dims = (1, 1, 0, 1, 1)
    norm_ada, norm_qkv, norm_proj, norm_up, norm_down = lax.psum(
        (
            jnp.sum(moment_ada * moment_ada),
            jnp.sum(moment_qkv * moment_qkv),
            jnp.sum(moment_proj * moment_proj),
            jnp.sum(moment_up * moment_up),
            jnp.sum(moment_down * moment_down),
        ),
        "tensor",
    )
    start_ada = (moment_ada / (jnp.sqrt(norm_ada) + 1e-07)).astype(jnp.bfloat16)
    start_qkv = (moment_qkv / (jnp.sqrt(norm_qkv) + 1e-07)).astype(jnp.bfloat16)
    start_proj = (moment_proj / (jnp.sqrt(norm_proj) + 1e-07)).astype(jnp.bfloat16)
    start_up = (moment_up / (jnp.sqrt(norm_up) + 1e-07)).astype(jnp.bfloat16)
    start_down = (moment_down / (jnp.sqrt(norm_down) + 1e-07)).astype(jnp.bfloat16)
    whole_starts = (
        lax.all_gather(start_ada, "tensor", axis=1, tiled=True),
        lax.all_gather(start_qkv, "tensor", axis=1, tiled=True),
        lax.all_gather(start_proj, "tensor", axis=0, tiled=True),
        lax.all_gather(start_up, "tensor", axis=1, tiled=True),
        lax.all_gather(start_down, "tensor", axis=1, tiled=True),
    )
    dp_size = lax.axis_size("dp")
    dp_rank = lax.axis_index("dp")
    owners = [matrix_index * (dp_size // 5) for matrix_index in range(5)]
    orienteds = tuple(
        (orient(whole_starts[matrix_index], matrix_index) for matrix_index in range(5))
    )
    selector = jnp.zeros((), jnp.int32)
    for matrix_index in range(5):
        selector = selector + jnp.where(
            dp_rank == owners[matrix_index], matrix_index + 1, 0
        ).astype(jnp.int32)
    branches = [make_branch(-1)] + [make_branch(matrix_index) for matrix_index in range(5)]
    orthos = lax.switch(selector, branches, orienteds)
    column_width = w_ada.shape[-1] // dp_size
    column_start = dp_rank * column_width
    weights_old = (w_ada, w_qkv, w_proj, w_up, w_down)
    new_weights = []
    for matrix_index in range(5):
        row_count, column_count = orienteds[matrix_index].shape
        restored = restore(orthos[matrix_index], matrix_index, whole_starts[matrix_index].shape)
        own_part = lax.dynamic_slice_in_dim(restored, offset, quarter, gather_dims[matrix_index])
        own_part = from_root(shortened(own_part), "dp", owners[matrix_index]).astype(own_part.dtype)
        last_axis = own_part.ndim - 1
        own_columns = lax.dynamic_slice_in_dim(own_part, column_start, column_width, last_axis)
        weight_columns = lax.dynamic_slice_in_dim(
            weights_old[matrix_index], column_start, column_width, last_axis
        )
        new_weights.append(
            weight_columns * (1.0 - MUON_RATE * MUON_DECAY)
            - MUON_RATE
            * 0.2
            * math.sqrt(max(row_count, column_count))
            * own_columns.astype(jnp.float32)
        )
    new_bias_first = BETA_ONE * bias_first + (1.0 - BETA_ONE) * grad_biases
    new_bias_second = BETA_TWO * bias_second + (1.0 - BETA_TWO) * grad_biases * grad_biases
    first_hat = new_bias_first / (1.0 - BETA_ONE**STEP)
    second_hat = new_bias_second / (1.0 - BETA_TWO**STEP)
    new_biases = biases - ADAM_RATE * first_hat / (jnp.sqrt(second_hat) + ADAM_EPS)
    return (
        output,
        grad_inputs,
        grad_condition,
        new_weights[0],
        new_weights[1],
        new_weights[2],
        new_weights[3],
        new_weights[4],
        moment_ada,
        moment_qkv,
        moment_proj,
        moment_up,
        moment_down,
        new_biases,
        new_bias_first,
        new_bias_second,
    )


def solution(mesh):
    placed = (
        P("dp", None, None),
        P("dp", None),
        P("dp", None, None),
        P(None, "tensor", None),
        P(None, "tensor", None),
        P("tensor", None),
        P(None, "tensor", None),
        P(None, "tensor", None),
        P(None, "tensor"),
        P(None, "tensor", None),
        P(None, "tensor", None),
        P("tensor", None),
        P(None, "tensor", None),
        P(None, "tensor", None),
        P(None, "tensor"),
        P(None, "tensor"),
    )
    return jax.shard_map(
        on_device,
        mesh=mesh,
        in_specs=placed,
        out_specs=(
            P("dp", None, None),
            P("dp", None, None),
            P("dp", None),
            P(None, "tensor", "dp"),
            P(None, "tensor", "dp"),
            P("tensor", "dp"),
            P(None, "tensor", "dp"),
            P(None, "tensor", "dp"),
            P(None, "tensor", None),
            P(None, "tensor", None),
            P("tensor", None),
            P(None, "tensor", None),
            P(None, "tensor", None),
            P(None, "tensor"),
            P(None, "tensor"),
            P(None, "tensor"),
        ),
        check_vma=False,
    )
```

profile of v0, /device:TPU:0, one launch (start us, length us, event | category | flops | bytes accessed | tf_op | source)
XLA Modules:
  0.0 1125.7 jit_solution(376605188811293270)
XLA Ops:
  12.1 2.6 convolution_add_fusion.1
  14.9 21.3 %all_gather.24 = f32[2,6,768]{1,0,2:T(2,128)S(1)} all-gather(f32[2,6,192]{1,0,2:T(2,128)S(1)} %copy.115), channel_id=1, replica_groups=mesh['dp'=8,'tensor'=4] {'tensor'}, dimensions={2}, use_global_device_ids=true | all-gather | bytes 46080 | tf_op jit(solution)/shard_map/all_gather | solution.py:126
  36.2 5.3 fusion.132
  42.3 2.3 fusion.83
  49.5 12.4 %all-gather = f32[4,192,2]{1,2,0:T(2,128)S(1)} all-gather(f32[1,192,2]{1,2,0:T(2,128)S(1)} %maximum_bitcast_fusion), channel_id=1, replica_groups=mesh['dp'=8,'tensor'=4] {'tensor'}, dimensions={0}, use_global_device_ids=true | all-gather | bytes 7680 | tf_op jit(solution)/shard_map/all_gather | solution.py:127
  63.8 1.9 copy.121
  65.7 1.9 copy.123
  67.6 1.9 copy.149
  72.5 18.8 %all-reduce.10.cloned.1.call-done = bf16[2,256,768]{2,1,0:T(8,128)(2,1)} async-done(((bf16[2,256,768]{2,1,0:T(8,128)(2,1)}), bf16[2,256,768]{2,1,0:T(8,128)(2,1)}) %all-reduce.10.cloned.1.call-update) | async-done | bytes 786448 | tf_op jit(solution)/shard_map/psum | solution.py:152
  96.7 2.4 fusion.136
  102.0 4.0 bitcast_convert_fusion.2
  106.0 38.9 %all-reduce.12.cloned.1.call-done = bf16[2,256,768]{2,1,0:T(8,128)(2,1)} async-done(((bf16[2,256,768]{2,1,0:T(8,128)(2,1)}), bf16[2,256,768]{2,1,0:T(8,128)(2,1)}) %all-reduce.12.cloned.1.call-update) | async-done | bytes 786448 | tf_op jit(solution)/shard_map/psum | solution.py:188
  144.9 1.8 fusion.62
  157.6 4.0 convolution_bitcast_fusion
  161.6 2.5 convolution_bitcast_fusion.1
  165.4 2.1 convolution_bitcast_fusion.2
  167.5 58.4 %all-reduce.18.cloned.1.call-done = (bf16[2,256,768]{2,1,0:T(8,128)(2,1)}, bf16[2,256,768]{2,1,0:T(8,128)(2,1)}) async-done(((bf16[2,256,768]{2,1,0:T(8,128)(2,1)}, bf16[2,256,768]{2,1,0:T(8,128)(2,1)}), (bf16[2,256,768]{2,1,0:T(8,128)(2,1)}, bf16[2,256,768]{2,1,0:T(8,128)(2,1)})) %all-reduce.18.cloned.1.call-update) | async-done | bytes 1572880 | tf_op jit(solution)/shard_map/psum | solution.py:168
  228.8 2.8 fusion.54
  231.6 2.7 fusion.122
  234.4 1.9 copy-done.4
  237.5 148.4 %all-reduce.14.cloned.1.call-done = (f32[6,192,768]{2,1,0:T(8,128)}, f32[3,192,768]{2,1,0:T(8,128)}, f32[192,768]{1,0:T(8,128)}, f32[4,192,768]{2,1,0:T(8,128)}, f32[4,192,768]{2,1,0:T(8,128)}) async-done(((f32[6,192,768]{2,1,0:T(8,128)}, f32[3,192,768]{2,1,0:T(8,128)}, f32[192,768]{1,0:T(8,128)}, f32[4,192,768]{2,1,0:T(8,128)}, f32[4,192,768]{2,1,0:T(8,128)}), (f32[6,192,768]{2,1,0:T(8,128)}, ...) | async-done | bytes 10616848 | tf_op jit(solution)/shard_map/psum | solution.py:266
  386.0 4.7 multiply_reduce_fusion
  393.5 2.2 multiply_reduce_fusion.3
  396.5 2.6 multiply_reduce_fusion.2
  399.8 2.6 multiply_reduce_fusion.1
  402.3 12.8 %all-reduce.1 = (f32[2,768]{1,0:T(2,128)}, f32[]{:T(128)}, f32[]{:T(128)}, f32[]{:T(128)}, f32[]{:T(128)}, /*index=5*/f32[]{:T(128)}) all-reduce(f32[2,768]{1,0:T(2,128)S(1)} %convolution_bitcast_fusion.5, f32[]{:T(128)} %get-tuple-element.74, f32[]{:T(128)} %get-tuple-element.72, ...), channel_id=1, replica_groups=mesh['dp'=8,'tensor'=4] {'tensor'}, use_global_device_ids=true, to_apply=%region_21.22 | all-reduce | flops 1541 | bytes 12328 | tf_op jit(solution)/shard_map/psum | solution.py:251
  415.8 2.5 divide_convert_fusion.3
  419.1 2.9 divide_convert_fusion.2
  422.7 3.1 divide_convert_fusion.1
  430.1 55.6 %all-gather.9.cloned.1.call-done = bf16[3,768,768]{2,1,0:T(8,128)(2,1)} async-done(((bf16[3,192,768]{2,1,0:T(8,128)(2,1)}), bf16[3,768,768]{2,1,0:T(8,128)(2,1)}) %all-gather.9.cloned.1.call-update) | async-done | bytes 3538960 | tf_op jit(solution)/shard_map/all_gather | solution.py:292
  485.7 5.8 copy.131
  491.5 83.8 %all-gather.13.cloned.1.call-done = bf16[4,768,768]{2,1,0:T(8,128)(2,1)} async-done(((bf16[4,192,768]{2,1,0:T(8,128)(2,1)}), bf16[4,768,768]{2,1,0:T(8,128)(2,1)}) %all-gather.13.cloned.1.call-update) | async-done | bytes 4718608 | tf_op jit(solution)/shard_map/all_gather | solution.py:294
  575.3 6.6 copy.132
  581.9 82.9 %all-gather.15.cloned.1.call-done = bf16[4,768,768]{2,1,0:T(8,128)(2,1)} async-done(((bf16[4,192,768]{2,1,0:T(8,128)(2,1)}), bf16[4,768,768]{2,1,0:T(8,128)(2,1)}) %all-gather.15.cloned.1.call-update) | async-done | bytes 4718608 | tf_op jit(solution)/shard_map/all_gather | solution.py:295
  664.8 6.6 copy.133
  671.4 121.7 %all-gather.7.cloned.1.call-done = bf16[6,768,768]{2,1,0:T(8,128)(2,1)} async-done(((bf16[6,192,768]{2,1,0:T(8,128)(2,1)}), bf16[6,768,768]{2,1,0:T(8,128)(2,1)}) %all-gather.7.cloned.1.call-update) | async-done | bytes 7077904 | tf_op jit(solution)/shard_map/all_gather | solution.py:291
  793.2 10.4 copy.130
  803.5 20.5 %all-gather.11.cloned.1.call-done = bf16[768,768]{1,0:T(8,128)(2,1)} async-done(((bf16[192,768]{1,0:T(8,128)(2,1)}), bf16[768,768]{1,0:T(8,128)(2,1)}) %all-gather.11.cloned.1.call-update) | async-done | bytes 1179664 | tf_op jit(solution)/shard_map/all_gather | solution.py:293
  824.0 153.5 %conditional.1 = (bf16[768,4608]{1,0:T(8,128)(2,1)}, bf16[768,2304]{1,0:T(8,128)(2,1)S(1)}, bf16[768,768]{1,0:T(8,128)(2,1)}, bf16[768,3072]{1,0:T(8,128)(2,1)}, bf16[768,3072]{1,0:T(8,128)(2,1)}) conditional(s32[]{:T(128)} %clamp.3, () %tuple.34, bf16[768,4608]{1,0:T(8,128)(2,1)} %bitcast.271, ...), branch_computations={%region_37.38_spmd, %region_38.39_spmd, %region_39.40_spmd, %regio... | conditional | flops 58976501760 | bytes 132120616 | solution.py:309
  824.2 10.8 convolution_convert_fusion.4
  835.0 13.4 %add_convert_fusion.4 = bf16[768,4608]{1,0:T(8,128)(2,1)} fusion(bf16[768,4608]{1,0:T(8,128)(2,1)} %param.1, bf16[768,768]{1,0:T(8,128)(2,1)S(1)} %convolution_convert_fusion.4), kind=kOutput, calls=%fused_computation.4 | convolution fusion | flops 6358892544 | bytes 15335424 | tf_op jit(solution)/shard_map/cond/branch_1_fun/dot_general | solution.py:58
  848.5 10.7 convolution_convert_fusion.3
  859.2 13.5 %add_convert_fusion.3 = bf16[768,4608]{1,0:T(8,128)(2,1)} fusion(bf16[768,4608]{1,0:T(8,128)(2,1)} %add_convert_fusion.4, bf16[768,768]{1,0:T(8,128)(2,1)S(1)} %convolution_convert_fusion.3), kind=kOutput, calls=%fused_computation.3 | convolution fusion | flops 6358892544 | bytes 15335424 | tf_op jit(solution)/shard_map/cond/branch_1_fun/dot_general | solution.py:58
  872.7 10.8 convolution_convert_fusion.2
  883.5 13.7 %add_convert_fusion.2 = bf16[768,4608]{1,0:T(8,128)(2,1)} fusion(bf16[768,4608]{1,0:T(8,128)(2,1)} %add_convert_fusion.3, bf16[768,768]{1,0:T(8,128)(2,1)S(1)} %convolution_convert_fusion.2), kind=kOutput, calls=%fused_computation.2 | convolution fusion | flops 6358892544 | bytes 15335424 | tf_op jit(solution)/shard_map/cond/branch_1_fun/dot_general | solution.py:58
  897.2 10.7 convolution_convert_fusion.1
  907.9 13.4 %add_convert_fusion.1 = bf16[768,4608]{1,0:T(8,128)(2,1)} fusion(bf16[768,4608]{1,0:T(8,128)(2,1)} %add_convert_fusion.2, bf16[768,768]{1,0:T(8,128)(2,1)S(1)} %convolution_convert_fusion.1), kind=kOutput, calls=%fused_computation.1 | convolution fusion | flops 6358892544 | bytes 15335424 | tf_op jit(solution)/shard_map/cond/branch_1_fun/dot_general | solution.py:58
  921.4 11.0 convolution_convert_fusion
  932.3 13.8 %add_convert_fusion = bf16[768,4608]{1,0:T(8,128)(2,1)} fusion(bf16[768,4608]{1,0:T(8,128)(2,1)} %add_convert_fusion.1, bf16[768,768]{1,0:T(8,128)(2,1)S(1)} %convolution_convert_fusion), kind=kOutput, calls=%fused_computation | convolution fusion | flops 6358892544 | bytes 15335424 | tf_op jit(solution)/shard_map/cond/branch_1_fun/dot_general | solution.py:58
  947.5 2.7 broadcast.188.clone
  950.2 2.7 broadcast.188
  977.6 10.3 copy.134
  987.9 3.0 dynamic-slice_select_fusion
  990.8 3.6 copy.135
  994.4 2.3 dynamic-slice_select_fusion.3
  998.5 6.6 copy.136
  1005.1 6.6 copy.137
  1011.7 3.5 dynamic-slice_select_fusion.1
  1017.9 24.1 %psum.167 = f32[14,192]{1,0:T(8,128)S(1)} all-reduce(f32[14,192]{1,0:T(8,128)S(1)} %concatenate.3), channel_id=1, replica_groups=mesh['dp'=8,'tensor'=4] {'dp'}, use_global_device_ids=true, to_apply=%region_54.55 | all-reduce | flops 2688 | bytes 21504 | tf_op jit(solution)/shard_map/psum | solution.py:266
  1043.3 64.4 %all-reduce.16.cloned.1.call-done = (bf16[6,192,768]{2,1,0:T(8,128)(2,1)}, bf16[3,192,768]{2,1,0:T(8,128)(2,1)}, bf16[192,768]{1,0:T(8,128)(2,1)}, bf16[4,192,768]{2,1,0:T(8,128)(2,1)}, bf16[4,192,768]{2,1,0:T(8,128)(2,1)}) async-done(((bf16[6,192,768]{2,1,0:T(8,128)(2,1)}, bf16[3,192,768]{2,1,0:T(8,128)(2,1)}, bf16[192,768]{1,0:T(8,128)(2,1)}, bf16[4,192,768]{2,1,0:T(8,128)(2,1)}, ...) | async-done | bytes 5308432 | tf_op jit(solution)/shard_map/psum | solution.py:32
  1107.7 2.5 multiply_subtract_fusion
  1111.9 2.0 multiply_subtract_fusion.3
  1114.0 2.2 multiply_subtract_fusion.2
  1116.2 2.2 multiply_subtract_fusion.1
  (273 shorter events, 55.4 us)
Async XLA Ops:
  7.2 84.1 %all-reduce.10.cloned.1.call-start = ((), (), s32[]{:S(2)}) async-start(), calls=%async_computation | async-start | bytes 1572864 | tf_op jit(solution)/shard_map/psum | solution.py:152
  10.6 31.7 %copy-start.52 = (f32[2,256]{1,0:T(2,128)}, f32[2,256]{1,0:T(2,128)S(1)}, u32[]{:S(2)}) copy-start(f32[2,256]{1,0:T(2,128)S(1)} %broadcast_multiply_fusion.1) | copy-start | bytes 6148
  12.1 2.6 copy-start.70
  12.1 30.1 %copy-start.74 = (f32[2,256]{1,0:T(2,128)}, f32[2,256]{1,0:T(2,128)S(1)}, u32[]{:S(2)}) copy-start(f32[2,256]{1,0:T(2,128)S(1)} %fusion.118) | copy-start | bytes 6148
  36.2 6.1 copy-start
  41.9 2.7 copy-start.44
  42.3 2.4 copy-start.81
  45.7 3.8 copy-start.87
  45.7 3.8 copy-start.88
  48.1 21.4 %copy-start.11 = (f32[2,1,768]{1,0,2:T(2,128)S(1)}, f32[2,1,768]{1,0,2:T(2,128)}, u32[]{:S(2)}) copy-start(f32[2,1,768]{1,0,2:T(2,128)} %get-tuple-element.86) | copy-start | bytes 18436
  48.1 96.8 %all-reduce.12.cloned.1.call-start = ((), (), s32[]{:S(2)}) async-start(), calls=%async_computation.1 | async-start | bytes 1572864 | tf_op jit(solution)/shard_map/psum | solution.py:188
  91.3 3.5 copy-start.32
  91.3 3.5 copy-start.41
  91.3 3.5 copy-start.46
  91.3 3.5 copy-start.83
  91.3 3.5 copy-start.86
  93.0 2.9 copy-start.49
  95.9 3.2 copy-start.93
  101.7 124.2 %all-reduce.18.cloned.1.call-start = ((), (), s32[]{:S(2)}) async-start(), calls=%async_computation.9 | async-start | bytes 3145728 | tf_op jit(solution)/shard_map/psum | solution.py:168
  151.7 2.9 copy-start.35
  153.3 2.0 copy-start.54
  153.6 3.3 copy-start.39
  155.3 2.2 copy-start.14
  155.3 2.2 copy-start.62
  157.0 229.0 %all-reduce.14.cloned.1.call-start = ((), (), s32[]{:S(2)}) async-start(), calls=%async_computation.7 | async-start | bytes 21233664 | tf_op jit(solution)/shard_map/psum | solution.py:266
  157.5 4.1 copy-start.34
  157.5 4.1 copy-start.43
  157.5 4.1 copy-start.51
  157.5 4.1 copy-start.69
  157.5 4.1 copy-start.84
  157.5 4.1 copy-start.92
  161.6 2.5 copy-start.3
  161.6 2.5 copy-start.28
  165.4 62.3 %copy-start.71 = (f32[2,256]{1,0:T(2,128)S(1)}, f32[2,256]{1,0:T(2,128)}, u32[]{:S(2)}) copy-start(f32[2,256]{1,0:T(2,128)} %copy-done.70) | copy-start | bytes 6148
  167.5 61.2 %copy-start.60 = (f32[2,768]{1,0:T(2,128)S(1)}, f32[2,768]{1,0:T(2,128)}, u32[]{:S(2)}) copy-start(f32[2,768]{1,0:T(2,128)} %get-tuple-element.36) | copy-start | bytes 18436
  167.5 61.2 %copy-start.59 = (f32[2,768]{1,0:T(2,128)S(1)}, f32[2,768]{1,0:T(2,128)}, u32[]{:S(2)}) copy-start(f32[2,768]{1,0:T(2,128)} %get-tuple-element.39) | copy-start | bytes 18436
  167.5 61.2 %copy-start.58 = (f32[2,768]{1,0:T(2,128)S(1)}, f32[2,768]{1,0:T(2,128)}, u32[]{:S(2)}) copy-start(f32[2,768]{1,0:T(2,128)} %get-tuple-element.31) | copy-start | bytes 18436
  167.5 61.2 %copy-start.76 = (f32[768]{0:T(1024)S(1)}, f32[768]{0:T(1024)}, u32[]{:S(2)}) copy-start(f32[768]{0:T(1024)} %get-tuple-element.43) | copy-start | bytes 9220
  226.0 2.8 copy-start.15
  226.0 2.8 copy-start.29
  228.8 2.8 copy-start.55
  231.6 2.7 copy-start.57
  234.3 2.0 copy-start.4
  234.4 251.3 %all-gather.9.cloned.1.call-start = ((), (), s32[]{:S(2)}) async-start(), calls=%async_computation.3 | async-start | bytes 4423680 | tf_op jit(solution)/shard_map/all_gather | solution.py:292
  386.0 4.8 copy-start.30
  386.0 4.8 copy-start.31
  386.0 6.3 copy-start.26
  390.7 35.9 %copy-start.5 = (f32[6,192,768]{2,1,0:T(8,128)}, f32[6,192,768]{2,1,0:T(8,128)S(1)}, u32[]{:S(2)}) copy-start(f32[6,192,768]{2,1,0:T(8,128)S(1)} %get-tuple-element.75) | copy-start | bytes 10616836
  390.7 2.8 copy-start.25
  393.5 2.3 copy-start.18
  393.5 3.0 copy-start.21
  396.5 2.6 copy-start.19
  396.5 3.2 copy-start.20
  418.3 156.9 %all-gather.13.cloned.1.call-start = ((), (), s32[]{:S(2)}) async-start(), calls=%async_computation.5 | async-start | bytes 5898240 | tf_op jit(solution)/shard_map/all_gather | solution.py:294
  422.0 242.8 %all-gather.15.cloned.1.call-start = ((), (), s32[]{:S(2)}) async-start(), calls=%async_computation.6 | async-start | bytes 5898240 | tf_op jit(solution)/shard_map/all_gather | solution.py:295
  425.8 367.3 %all-gather.7.cloned.1.call-start = ((), (), s32[]{:S(2)}) async-start(), calls=%async_computation.2 | async-start | bytes 8847360 | tf_op jit(solution)/shard_map/all_gather | solution.py:291
  428.1 395.9 %all-gather.11.cloned.1.call-start = ((), (), s32[]{:S(2)}) async-start(), calls=%async_computation.4 | async-start | bytes 1474560 | tf_op jit(solution)/shard_map/all_gather | solution.py:293
  430.0 677.7 %all-reduce.16.cloned.1.call-start = ((), (), s32[]{:S(2)}) async-start(), calls=%async_computation.8 | async-start | bytes 10616832 | tf_op jit(solution)/shard_map/psum | solution.py:32
  1015.3 2.6 copy-start.89
  1015.3 26.7 %copy-start.48 = (f32[14,192]{1,0:T(8,128)S(1)}, f32[14,192]{1,0:T(8,128)}, u32[]{:S(2)}) copy-start(f32[14,192]{1,0:T(8,128)} %param.30) | copy-start | bytes 32260
  1015.3 26.7 %copy-start.77 = (f32[14,192]{1,0:T(8,128)S(1)}, f32[14,192]{1,0:T(8,128)}, u32[]{:S(2)}) copy-start(f32[14,192]{1,0:T(8,128)} %param.36) | copy-start | bytes 32260
  1015.3 26.7 %copy-start.78 = (f32[14,192]{1,0:T(8,128)S(1)}, f32[14,192]{1,0:T(8,128)}, u32[]{:S(2)}) copy-start(f32[14,192]{1,0:T(8,128)} %param.37) | copy-start | bytes 32260
  1015.3 27.3 %copy-start.56 = (bf16[2,768]{1,0:T(2,128)(2,1)S(1)}, bf16[2,768]{1,0:T(2,128)(2,1)}, u32[]{:S(2)}) copy-start(bf16[2,768]{1,0:T(2,128)(2,1)} %param.23) | copy-start | bytes 9220
  1015.3 27.3 %copy-start.85 = (f32[2,768]{1,0:T(2,128)S(1)}, f32[2,768]{1,0:T(2,128)}, u32[]{:S(2)}) copy-start(f32[2,768]{1,0:T(2,128)} %get-tuple-element.50) | copy-start | bytes 18436
  (38 other events, 49.6 us)
Sparse Core Ops, SparseCore 0:
  48.2 43.0 all-reduce.9
  101.8 42.9 all-reduce.11
  157.1 68.7 all-reduce.17
  234.5 151.4 all-reduce.13
  418.5 67.1 all-gather.8
  487.2 88.0 all-gather.12
  576.9 87.8 all-gather.14
  666.5 126.6 all-gather.6
  795.4 28.6 all-gather.10
  1015.5 92.1 all-reduce.15
where the time goes:
time: 1140 us; the launch traced here: 1130 us
  waiting for transfers between devices  694 us (61%)
  matrix products  157 us (14%)
  local copies, waits for them, and re-layouts  93.8 us (8%)
  blocking collectives  70.5 us (6%)
  other arithmetic  66.1 us (6%)
  loops' own time  24.9 us (2%)
  between operations  19.1 us (2%)
    psum x1, waiting for transfers between devices, on_device(): lax.psum((grad_ada, grad_qkv, grad_proj, grad_up, grad_down, grad_biases)...  148 us
    all_gather x1, waiting for transfers between devices, on_device(): lax.all_gather(start_ada, 'tensor', axis=1, tiled=True)  122 us
    all_gather x1, waiting for transfers between devices, on_device(): lax.all_gather(start_up, 'tensor', axis=1, tiled=True)  83.8 us
    all_gather x1, waiting for transfers between devices, on_device(): lax.all_gather(start_down, 'tensor', axis=1, tiled=True)  82.9 us
    dot_general x5, matrix products, orthogonalize(): product = jnp.dot(poly, current, preferred_element_type=jnp.float32)  67.8 us
    psum x1, waiting for transfers between devices, from_root(): return lax.psum(block, axis)  64.4 us
    psum x1, waiting for transfers between devices, on_device(): lax.psum(partial_second.astype(jnp.bfloat16), 'tensor').astype(jnp.float32)  58.4 us
    all_gather x1, waiting for transfers between devices, on_device(): lax.all_gather(start_qkv, 'tensor', axis=1, tiled=True)  55.6 us
  transfers between devices with their start and end apart: 10, of which 10 were waited for; matrix products, arithmetic and copies ran while one was open for 6% of the time, Pallas kernels for 0%

commit v1 on v0

v1 whole, which is shorter than its diff:
```python
import math

import jax
import jax.numpy as jnp
from jax import lax
from jax.sharding import PartitionSpec as P

HEAD_DIM = 64
NS_ITERS = 5
STEP = 10


NS_A = 3.4445
NS_B = -4.775
NS_C = 2.0315
MUON_RATE = 0.16
MUON_DECAY = 0.01
MUON_MOMENTUM = 0.95
ADAM_RATE = 0.25
BETA_ONE = 0.9
BETA_TWO = 0.999
ADAM_EPS = 1e-08
NORM_EPS = 1e-06

BF = jnp.bfloat16
F32 = jnp.float32
TILE = 256
OWNERS = (0, 2, 1, 4, 6)


def layer_norm(values):
    average = jnp.mean(values, axis=-1, keepdims=True)
    centered = values - average
    variance = jnp.mean(centered * centered, axis=-1, keepdims=True)
    return centered * lax.rsqrt(variance + NORM_EPS)


def modulate(values, shift_by, scale_by):
    return layer_norm(values) * (1.0 + scale_by[:, None, :]) + shift_by[:, None, :]


def gelu_tanh(values):
    return jax.nn.gelu(values, approximate=True)


def dot(a, b):
    return jnp.dot(a, b, preferred_element_type=F32)


def dot_t(a, b):
    return lax.dot_general(a, b, (((1,), (1,)), ((), ())), preferred_element_type=F32)


def t_dot(a, b):
    return lax.dot_general(a, b, (((0,), (0,)), ((), ())), preferred_element_type=F32)


def parts(value):
    high = value.astype(BF)
    return high, (value - high.astype(F32)).astype(BF)


def newton_schulz_factor(gram):
    width = gram.shape[0]
    eye = jnp.eye(width, dtype=F32)
    scale = 1.0 / (jnp.sqrt(jnp.sum(gram * eye)) + 1e-07)
    current = gram * (scale * scale)
    factor = None
    for iteration in range(NS_ITERS):
        low = current.astype(BF)
        poly = (NS_B * current + NS_C * dot(low, low)).astype(BF)
        if factor is None:
            factor = NS_A * eye + poly.astype(F32)
        else:
            high, rest = parts(factor)
            factor = NS_A * factor + dot(high, poly) + dot(rest, poly)
        if iteration < NS_ITERS - 1:
            high, rest = parts(current)
            half = NS_A * current + dot(high, poly) + dot(rest, poly)
            high, rest = parts(half)
            current = NS_A * half + dot(poly, high) + dot(poly, rest)
    return factor * scale


def pack(gram):
    count = gram.shape[0] // TILE
    return jnp.stack(
        [
            gram[i * TILE : (i + 1) * TILE, j * TILE : (j + 1) * TILE]
            for i in range(count)
            for j in range(i, count)
        ]
    )


def unpack(blocks, width):
    count = width // TILE
    index = {}
    for i in range(count):
        for j in range(i, count):
            index[i, j] = len(index)
    rows = []
    for i in range(count):
        rows.append(
            jnp.concatenate(
                [blocks[index[i, j]] if j >= i else blocks[index[j, i]].T for j in range(count)], axis=1
            )
        )
    return jnp.concatenate(rows, axis=0)


def on_device(
    inputs,
    condition,
    cotangent,
    w_ada,
    w_qkv,
    w_proj,
    w_up,
    w_down,
    biases,
    momentum_ada,
    momentum_qkv,
    momentum_proj,
    momentum_up,
    momentum_down,
    bias_first,
    bias_second,
):
    quarter = w_ada.shape[1]
    width = w_ada.shape[-1]
    latent_count = inputs.shape[0]
    seq_length = inputs.shape[1]
    tokens = latent_count * seq_length
    heads_here = quarter // HEAD_DIM
    offset = lax.axis_index("tensor") * quarter
    scale_factor = 1.0 / math.sqrt(HEAD_DIM)
    flat = lambda w: w.reshape(-1, width)
    ada_low = flat(w_ada).astype(BF)
    qkv_low = flat(w_qkv).astype(BF)
    proj_low = w_proj.astype(BF)
    up_low = flat(w_up).astype(BF)
    down_low = flat(w_down).astype(BF)
    up_bias = biases[9:13].reshape(-1)

    cond_act, silu_pull = jax.vjp(jax.nn.silu, condition.astype(F32))
    cond_low = cond_act.astype(BF)
    mod_part = dot_t(cond_low, ada_low).reshape(latent_count, 6, quarter) + biases[0:6]
    mod_part = jnp.concatenate(
        [mod_part.reshape(-1, quarter), biases[8:9], biases[13:14]], axis=0
    )
    gathered = lax.all_gather(mod_part, "tensor", axis=1, tiled=True)
    modulation = gathered[: latent_count * 6].reshape(latent_count, 6, width)
    out_bias = gathered[latent_count * 6 :]

    inputs_f = inputs.astype(F32)
    hidden_first, first_pull = jax.vjp(modulate, inputs_f, modulation[:, 0], modulation[:, 1])
    first_low = hidden_first.astype(BF).reshape(tokens, width)
    projected = dot_t(first_low, qkv_low)
    head_shape = (latent_count, seq_length, heads_here, HEAD_DIM)
    query_heads = (projected[:, :quarter] + biases[6]).astype(BF).reshape(head_shape)
    key_heads = projected[:, quarter : 2 * quarter].astype(BF).reshape(head_shape)
    value_heads = (projected[:, 2 * quarter :] + biases[7]).astype(BF).reshape(head_shape)
    scores = (
        jnp.einsum("bqhc,bkhc->bhqk", query_heads, key_heads, preferred_element_type=F32)
        * scale_factor
    )
    row_top = jnp.max(scores, axis=-1, keepdims=True)
    log_total = row_top + jnp.log(jnp.sum(jnp.exp(scores - row_top), axis=-1, keepdims=True))
    probs_low = jnp.exp(scores - log_total).astype(BF)
    attended = jnp.einsum("bhqk,bkhc->bqhc", probs_low, value_heads, preferred_element_type=F32)
    attended_low = attended.reshape(tokens, quarter).astype(BF)
    partial_first = dot(attended_low, proj_low).reshape(latent_count, seq_length, width)
    branch_first = lax.psum(partial_first.astype(BF), "tensor").astype(F32) + out_bias[0]
    gate_first = modulation[:, 2][:, None, :]
    middle = inputs_f + gate_first * branch_first
    hidden_second, second_pull = jax.vjp(modulate, middle, modulation[:, 3], modulation[:, 4])
    second_low = hidden_second.astype(BF).reshape(tokens, width)
    pre_act = dot_t(second_low, up_low) + up_bias
    activated, gelu_pull = jax.vjp(gelu_tanh, pre_act)
    act_low = activated.astype(BF)

    gate_second = modulation[:, 5][:, None, :]
    tangent = cotangent.astype(F32)
    d_branch_second = gate_second * tangent
    d_down_bias = jnp.sum(d_branch_second, axis=(0, 1))
    d_second_low = d_branch_second.astype(BF).reshape(tokens, width)
    d_act = dot_t(d_second_low, down_low)
    d_pre = gelu_pull(d_act)[0]
    d_up_bias = jnp.sum(d_pre, axis=0).reshape(-1, quarter)
    d_pre_low = d_pre.astype(BF)
    d_second_part = dot(d_pre_low, up_low).astype(BF)
    d_second_sum = lax.psum(d_second_part, "tensor")

    partial_second = dot(act_low, down_low).astype(BF)
    partial_second, d_second_sum = lax.optimization_barrier((partial_second, d_second_sum))
    second_sum = lax.psum(partial_second, "tensor")

    grad_down = t_dot(act_low, d_second_low).astype(BF)
    grad_up = t_dot(d_pre_low, second_low).astype(BF)
    grad_up, grad_down = lax.psum((grad_up, grad_down), "dp")

    d_hidden_second = d_second_sum.reshape(latent_count, seq_length, width).astype(F32)
    d_middle_norm, d_shift_second, d_scale_second = second_pull(d_hidden_second)
    d_middle = tangent + d_middle_norm
    d_branch_first = gate_first * d_middle
    d_gate_first = jnp.sum(d_middle * branch_first, axis=1)
    d_proj_bias = jnp.sum(d_branch_first, axis=(0, 1))
    d_first_low = d_branch_first.astype(BF).reshape(tokens, width)
    grad_proj = t_dot(attended_low, d_first_low).astype(BF)
    d_attended = dot_t(d_first_low, proj_low).astype(BF).reshape(head_shape)
    probs = jnp.exp(scores - log_total)
    probs_again = probs.astype(BF)
    d_values = jnp.einsum("bhqk,bqhc->bkhc", probs_again, d_attended, preferred_element_type=F32)
    d_probs = jnp.einsum("bqhc,bkhc->bhqk", d_attended, value_heads, preferred_element_type=F32)
    d_scores = (probs * (d_probs - jnp.sum(probs * d_probs, axis=-1, keepdims=True))).astype(BF)
    d_queries = (
        jnp.einsum("bhqk,bkhc->bqhc", d_scores, key_heads, preferred_element_type=F32)
        * scale_factor
    )
    d_keys = (
        jnp.einsum("bhqk,bqhc->bkhc", d_scores, query_heads, preferred_element_type=F32)
        * scale_factor
    )
    d_queries = d_queries.reshape(tokens, quarter)
    d_keys = d_keys.reshape(tokens, quarter)
    d_values = d_values.reshape(tokens, quarter)
    d_query_bias = jnp.sum(d_queries, axis=0)
    d_value_bias = jnp.sum(d_values, axis=0)
    d_projected_low = jnp.concatenate([d_queries, d_keys, d_values], axis=1).astype(BF)
    d_first_part = dot(d_projected_low, qkv_low).astype(BF)

    d_first_part, second_sum = lax.optimization_barrier((d_first_part, second_sum))
    d_hidden_first = (
        lax.psum(d_first_part, "tensor").reshape(latent_count, seq_length, width).astype(F32)
    )
    branch_second = (
        second_sum.reshape(latent_count, seq_length, width).astype(F32) + out_bias[1]
    )
    output = (middle + gate_second * branch_second).astype(BF)
    d_gate_second = jnp.sum(tangent * branch_second, axis=1)

    grad_qkv = t_dot(d_projected_low, first_low).astype(BF)
    grad_qkv, grad_proj, grad_up, grad_down = lax.optimization_barrier(
        (grad_qkv, grad_proj, grad_up, grad_down)
    )
    grad_qkv, grad_proj = lax.psum((grad_qkv, grad_proj), "dp")

    d_inputs_norm, d_shift_first, d_scale_first = first_pull(d_hidden_first)
    grad_inputs = (d_middle + d_inputs_norm).astype(BF)
    d_modulation = jnp.stack(
        [d_shift_first, d_scale_first, d_gate_first, d_shift_second, d_scale_second, d_gate_second],
        axis=1,
    )
    d_mod_own = lax.dynamic_slice_in_dim(d_modulation, offset, quarter, 2)
    d_cond_part = dot(d_mod_own.reshape(latent_count, -1).astype(BF), ada_low)
    d_proj_own = lax.dynamic_slice_in_dim(d_proj_bias, offset, quarter, 0)
    d_down_own = lax.dynamic_slice_in_dim(d_down_bias, offset, quarter, 0)
    small = jnp.concatenate(
        [
            d_mod_own.reshape(-1, quarter),
            d_query_bias[None],
            d_value_bias[None],
            d_proj_own[None],
            d_up_bias,
            d_down_own[None],
        ],
        axis=0,
    )
    cond_all = lax.all_gather(cond_low, "dp", axis=0, tiled=True)
    small_all = lax.all_gather(small, "dp", axis=0)
    d_mod_all = small_all[:, : 6 * latent_count].reshape(-1, 6, quarter)
    grad_biases = jnp.concatenate(
        [jnp.sum(d_mod_all, axis=0), jnp.sum(small_all[:, 6 * latent_count :], axis=0)], axis=0
    )
    grad_ada = t_dot(d_mod_all.reshape(d_mod_all.shape[0], -1).astype(BF), cond_all)
    d_cond_act = lax.psum(d_cond_part, "tensor")
    grad_condition = silu_pull(d_cond_act)[0]

    moments = (
        MUON_MOMENTUM * flat(momentum_ada) + grad_ada,
        MUON_MOMENTUM * flat(momentum_qkv) + grad_qkv.astype(F32),
        MUON_MOMENTUM * momentum_proj + grad_proj.astype(F32),
        MUON_MOMENTUM * flat(momentum_up) + grad_up.astype(F32),
        MUON_MOMENTUM * flat(momentum_down) + grad_down.astype(F32),
    )
    starts = tuple(m.astype(BF) for m in moments)

    dp_size = lax.axis_size("dp")
    dp_rank = lax.axis_index("dp")
    chosen = jnp.int32(2)
    for matrix_index, owner in enumerate(OWNERS):
        chosen = jnp.where(dp_rank == owner, matrix_index, chosen)
    gram_of = [
        (lambda kept, matrix_index=matrix_index: t_dot(kept[matrix_index], kept[matrix_index]))
        for matrix_index in range(5)
    ]
    gram = lax.switch(chosen, gram_of, starts)
    gram = unpack(lax.psum(pack(gram), "tensor"), width)
    factor = newton_schulz_factor(gram).astype(BF)
    column_width = width // dp_size
    column_start = dp_rank * column_width
    pieces = jnp.moveaxis(factor.reshape(width, dp_size, column_width), 1, 0)
    factors = lax.all_to_all(pieces, "dp", 0, 0, tiled=True)

    weights_old = (w_ada, w_qkv, w_proj, w_up, w_down)
    new_weights = []
    for matrix_index, weight in enumerate(weights_old):
        rows = weight.size // width * lax.axis_size("tensor")
        ortho = dot(starts[matrix_index], factors[OWNERS[matrix_index]])
        weight_columns = lax.dynamic_slice_in_dim(flat(weight), column_start, column_width, 1)
        updated = (
            weight_columns * (1.0 - MUON_RATE * MUON_DECAY)
            - MUON_RATE * 0.2 * math.sqrt(max(rows, width)) * ortho
        )
        new_weights.append(updated.reshape(weight.shape[:-1] + (column_width,)))
    new_bias_first = BETA_ONE * bias_first + (1.0 - BETA_ONE) * grad_biases
    new_bias_second = BETA_TWO * bias_second + (1.0 - BETA_TWO) * grad_biases * grad_biases
    first_hat = new_bias_first / (1.0 - BETA_ONE**STEP)
    second_hat = new_bias_second / (1.0 - BETA_TWO**STEP)
    new_biases = biases - ADAM_RATE * first_hat / (jnp.sqrt(second_hat) + ADAM_EPS)
    return (
        output,
        grad_inputs,
        grad_condition,
        *new_weights,
        moments[0].reshape(momentum_ada.shape),
        moments[1].reshape(momentum_qkv.shape),
        moments[2],
        moments[3].reshape(momentum_up.shape),
        moments[4].reshape(momentum_down.shape),
        new_biases,
        new_bias_first,
        new_bias_second,
    )


def solution(mesh):
    placed = (
        P("dp", None, None),
        P("dp", None),
        P("dp", None, None),
        P(None, "tensor", None),
        P(None, "tensor", None),
        P("tensor", None),
        P(None, "tensor", None),
        P(None, "tensor", None),
        P(None, "tensor"),
        P(None, "tensor", None),
        P(None, "tensor", None),
        P("tensor", None),
        P(None, "tensor", None),
        P(None, "tensor", None),
        P(None, "tensor"),
        P(None, "tensor"),
    )
    return jax.shard_map(
        on_device,
        mesh=mesh,
        in_specs=placed,
        out_specs=(
            P("dp", None, None),
            P("dp", None, None),
            P("dp", None),
            P(None, "tensor", "dp"),
            P(None, "tensor", "dp"),
            P("tensor", "dp"),
            P(None, "tensor", "dp"),
            P(None, "tensor", "dp"),
            P(None, "tensor", None),
            P(None, "tensor", None),
            P("tensor", None),
            P(None, "tensor", None),
            P(None, "tensor", None),
            P(None, "tensor"),
            P(None, "tensor"),
            P(None, "tensor"),
        ),
        check_vma=False,
    )
```

time: 1140 us -> 590 us (0.52)
  waiting for transfers between devices: 694 us -> 301 us
  matrix products: 157 us -> 92.4 us
  blocking collectives: 70.5 us -> 43.5 us
  loops' own time: 24.9 us -> 0.15 us
  local copies, waits for them, and re-layouts: 93.8 us -> 69.4 us
  other arithmetic: 66.1 us -> 53.1 us
    all_gather x5 -> x0, waiting for transfers between devices: 365 us -> none  [the longest x1 122 us: on_device(): lax.all_gather(start_ada, 'tensor', axis=1, tiled=True)]
    dot_general x25 -> x50, matrix products: 153 us -> 86.6 us  [the longest x39 58.6 us: dot(): return jnp.dot(a, b, preferred_element_type=F32)]
    psum x5 -> x7, waiting for transfers between devices: 329 us -> 300 us  [the longest x1 67.5 us: on_device(): gram = unpack(lax.psum(pack(gram), 'tensor'), width)]
    transpose x4 -> x1, local copies, waits for them, and re-layouts: 27.1 us -> 1.79 us  [unpack(): blocks[index[j, i]]]
    reshape x4 -> x9, local copies, waits for them, and re-layouts: 29.5 us -> 4.37 us  [the longest x1 1.57 us: on_device(): d_mod_all = small_all[:, :6 * latent_count].reshape(-1, 6, quarter)]
    another operation x1, loops' own time: 24.9 us -> 0.15 us  [on_device(): gram = lax.switch(chosen, gram_of, starts)]
    unnamed x192, local copies, waits for them, and re-layouts: 13 us -> 37.3 us
    psum x1 -> x0, blocking collectives: 24.1 us -> none  [on_device(): lax.psum((grad_ada, grad_qkv, grad_proj, grad_up, grad_down, grad_biases)...]
  transfers between devices with their start and end apart: 10 -> 8, of which waited for: 10 -> 8; matrix products, arithmetic and copies ran while one was open for 6% -> 15% of each run, Pallas kernels for 0% -> 0%
where the time goes in v1:
time: 590 us; the launch traced here: 581 us
  waiting for transfers between devices  301 us (51%)
  matrix products  92.4 us (16%)
  local copies, waits for them, and re-layouts  69.4 us (12%)
  other arithmetic  53.1 us (9%)
  blocking collectives  43.5 us (7%)
  between operations  16.5 us (3%)
    psum x1, waiting for transfers between devices, on_device(): gram = unpack(lax.psum(pack(gram), 'tensor'), width)  67.5 us
    dot_general x39, matrix products, dot(): return jnp.dot(a, b, preferred_element_type=F32)  58.6 us
    psum x1, waiting for transfers between devices, on_device(): grad_qkv, grad_proj = lax.psum((grad_qkv, grad_proj), 'dp')  56.4 us
    psum x1, waiting for transfers between devices, on_device(): lax.psum(d_first_part, 'tensor').reshape(latent_count, seq_length, width)  40.5 us
    psum x1, waiting for transfers between devices, on_device(): second_sum = lax.psum(partial_second, 'tensor')  39.6 us
    psum x1, waiting for transfers between devices, on_device(): grad_up, grad_down = lax.psum((grad_up, grad_down), 'dp')  39.2 us
    unnamed x192, local copies, waits for them, and re-layouts  37.3 us
    psum x1, waiting for transfers between devices, on_device(): d_second_sum = lax.psum(d_second_part, 'tensor')  31.1 us
  transfers between devices with their start and end apart: 8, of which 8 were waited for; matrix products, arithmetic and copies ran while one was open for 15% of the time, Pallas kernels for 0%

profile of v1, /device:TPU:0, one launch (start us, length us, event | category | flops | bytes accessed | tf_op | source)
XLA Modules:
  0.0 581.2 jit_solution(10538904494905572032)
XLA Ops:
  8.7 2.6 convolution_add_fusion.2
  11.4 15.0 %all-gather.1 = f32[4,192,14]{1,2,0:T(8,128)S(1)} all-gather(f32[1,192,14]{1,2,0:T(8,128)S(1)} %maximum_bitcast_fusion), channel_id=1, replica_groups=mesh['dp'=8,'tensor'=4] {'tensor'}, dimensions={0}, use_global_device_ids=true | all-gather | bytes 53760 | tf_op jit(solution)/shard_map/all_gather | solution.py:152
  33.7 1.9 convert_element_type.368
  36.1 1.6 broadcast_multiply_fusion.1
  40.5 2.0 fusion.143
  47.3 3.5 broadcast_multiply_fusion.2
  50.8 2.1 broadcast_multiply_fusion
  52.9 25.7 %all-reduce.10.cloned.1.call-done = bf16[2,256,768]{2,1,0:T(8,128)(2,1)} async-done(((bf16[2,256,768]{2,1,0:T(8,128)(2,1)}), bf16[2,256,768]{2,1,0:T(8,128)(2,1)}) %all-reduce.10.cloned.1.call-update) | async-done | bytes 786448 | tf_op jit(solution)/shard_map/psum | solution.py:174
  82.1 2.8 fusion.127
  85.9 1.7 convolution_convert_fusion.3
  87.8 3.2 convolution_convert_fusion.1
  91.7 3.8 convolution_convert_fusion
  95.5 4.1 convolution_convert_fusion.4
  99.6 31.1 %all-reduce.12.cloned.1.call-done = bf16[512,768]{1,0:T(8,128)(2,1)} async-done(((bf16[512,768]{1,0:T(8,128)(2,1)}), bf16[512,768]{1,0:T(8,128)(2,1)}) %all-reduce.12.cloned.1.call-update) | async-done | bytes 786448 | tf_op jit(solution)/shard_map/psum | solution.py:193
  130.7 3.0 fusion.25
  133.8 1.8 add_add_fusion.1
  137.2 2.1 multiply_convert_fusion.4
  154.2 3.0 convolution_convert_fusion.2
  157.2 39.2 %all-reduce.22.cloned.1.call-done = (bf16[768,768]{1,0:T(8,128)(2,1)}, bf16[768,768]{1,0:T(8,128)(2,1)}) async-done(((bf16[768,768]{1,0:T(8,128)(2,1)}, bf16[768,768]{1,0:T(8,128)(2,1)}), (bf16[768,768]{1,0:T(8,128)(2,1)}, bf16[768,768]{1,0:T(8,128)(2,1)})) %all-reduce.22.cloned.1.call-update) | async-done | bytes 2359312 | tf_op jit(solution)/shard_map/psum | solution.py:201
  196.5 2.9 convolution_convert_fusion.5
  199.4 3.5 fusion.123
  202.9 39.6 %all-reduce.14.cloned.1.call-done = bf16[512,768]{1,0:T(8,128)(2,1)} async-done(((bf16[512,768]{1,0:T(8,128)(2,1)}), bf16[512,768]{1,0:T(8,128)(2,1)}) %all-reduce.14.cloned.1.call-update) | async-done | bytes 786448 | tf_op jit(solution)/shard_map/psum | solution.py:197
  242.9 3.8 fusion.124
  246.7 56.4 %all-reduce.20.cloned.1.call-done = (bf16[576,768]{1,0:T(8,128)(2,1)}, bf16[192,768]{1,0:T(8,128)(2,1)}) async-done(((bf16[576,768]{1,0:T(8,128)(2,1)}, bf16[192,768]{1,0:T(8,128)(2,1)}), (bf16[576,768]{1,0:T(8,128)(2,1)}, bf16[192,768]{1,0:T(8,128)(2,1)})) %all-reduce.20.cloned.1.call-update) | async-done | bytes 1179664 | tf_op jit(solution)/shard_map/psum | solution.py:247
  303.1 2.1 fusion.125
  305.2 2.9 fusion.126
  308.2 40.5 %all-reduce.16.cloned.1.call-done = bf16[2,256,768]{2,1,0:T(8,128)(2,1)} async-done(((bf16[2,256,768]{2,1,0:T(8,128)(2,1)}), bf16[2,256,768]{2,1,0:T(8,128)(2,1)}) %all-reduce.16.cloned.1.call-update) | async-done | bytes 786448 | tf_op jit(solution)/shard_map/psum | solution.py:235
  348.6 1.7 fusion.22
  350.4 2.0 fusion.24
  352.5 3.7 multiply_reduce_fusion.3
  357.3 9.2 %all-gather.2 = f32[8,20,192]{2,1,0:T(8,128)S(1)} all-gather(f32[1,20,192]{2,1,0:T(8,128)S(1)} %bitcast.282), channel_id=2, replica_groups=mesh['dp'=8,'tensor'=4] {'dp'}, dimensions={0}, use_global_device_ids=true | all-gather | bytes 138240 | tf_op jit(solution)/shard_map/all_gather | solution.py:271
  366.6 10.3 %psum.74 = f32[2,768]{1,0:T(2,128)S(1)} all-reduce(f32[2,768]{1,0:T(2,128)S(1)} %convolution_bitcast_fusion.1), channel_id=1, replica_groups=mesh['dp'=8,'tensor'=4] {'tensor'}, use_global_device_ids=true, to_apply=%region_21.22 | all-reduce | flops 1536 | bytes 12288 | tf_op jit(solution)/shard_map/psum | solution.py:277
  377.5 9.0 %all-gather.3 = bf16[8,2,768]{2,1,0:T(2,128)(2,1)S(1)} all-gather(bf16[1,2,768]{2,1,0:T(2,128)(2,1)S(1)} %get-tuple-element.247), channel_id=1, replica_groups=mesh['dp'=8,'tensor'=4] {'dp'}, dimensions={0}, use_global_device_ids=true | all-gather | bytes 27648 | tf_op jit(solution)/shard_map/all_gather | solution.py:270
  386.6 4.6 fusion.136
  391.1 3.3 conditional.1
  391.1 3.2 fusion.137
  394.5 2.4 fusion.129
  396.9 1.8 copy.232
  398.7 1.7 bitcast_dynamic-update-slice_fusion.5
  400.3 1.8 copy.233
  402.1 1.8 copy.234
  403.9 1.8 copy.235
  405.7 1.8 copy.236
  408.3 1.7 bitcast_dynamic-update-slice_fusion.4
  410.0 1.7 bitcast_dynamic-update-slice_fusion.3
  411.7 1.7 bitcast_dynamic-update-slice_fusion.2
  414.8 67.5 %all-reduce.18.cloned.1.call-done = f32[6,256,256]{1,2,0:T(8,128)} async-done(((f32[6,256,256]{1,2,0:T(8,128)}), f32[6,256,256]{1,2,0:T(8,128)}) %all-reduce.18.cloned.1.call-update) | async-done | bytes 1572880 | tf_op jit(solution)/shard_map/psum | solution.py:299
  482.4 2.5 fusion.130
  486.8 1.8 copy.240
  488.6 2.0 pad_maximum_fusion
  490.5 2.3 copy.171
  492.9 1.8 copy.170
  494.6 2.2 select_reduce_fusion
  497.7 4.1 add_convert_fusion.4
  533.2 2.2 multiply_convert_fusion
  535.4 4.3 all-to-all-start
  546.1 2.3 constant_dynamic-slice_fusion.3
  556.5 2.6 fusion.43
  559.1 1.9 copy.224
  561.0 2.6 fusion.44
  563.6 1.9 copy.223
  565.5 2.1 fusion.45
  567.6 1.8 copy.194
  572.1 1.9 fusion.47
  (301 shorter events, 93.1 us)
Async XLA Ops:
  7.2 71.4 %all-reduce.10.cloned.1.call-start = ((), (), s32[]{:S(2)}) async-start(), calls=%async_computation.1 | async-start | bytes 1572864 | tf_op jit(solution)/shard_map/psum | solution.py:174
  8.7 18.5 %copy-start = (bf16[2,256,768]{2,1,0:T(8,128)(2,1)S(1)}, bf16[2,256,768]{2,1,0:T(8,128)(2,1)}, u32[]{:S(2)}) copy-start(bf16[2,256,768]{2,1,0:T(8,128)(2,1)} %param.21) | copy-start | bytes 2359300
  11.4 16.5 %copy-start.7 = (f32[3,192,768]{2,1,0:T(8,128)S(1)}, f32[3,192,768]{2,1,0:T(8,128)}, u32[]{:S(2)}) copy-start(f32[3,192,768]{2,1,0:T(8,128)} %param.25) | copy-start | bytes 5308420
  32.0 1.7 copy-start.28
  33.7 97.0 %all-reduce.12.cloned.1.call-start = ((), (), s32[]{:S(2)}) async-start(), calls=%async_computation.2 | async-start | bytes 1572864 | tf_op jit(solution)/shard_map/psum | solution.py:193
  33.7 2.4 copy-start.23
  36.1 2.2 copy-start.25
  38.3 2.0 copy-start.14
  39.7 2.8 copy-start.53
  40.5 2.0 copy-start.41
  40.5 4.1 copy-start.4
  47.3 3.5 copy-start.17
  50.8 27.8 %copy-start.45 = (f32[768]{0:T(1024)S(1)}, f32[768]{0:T(1024)}, u32[]{:S(2)}) copy-start(f32[768]{0:T(1024)} %get-tuple-element.198) | copy-start | bytes 9220
  78.6 2.2 copy-start.49
  78.6 2.2 copy-start.63
  81.3 3.6 copy-start.42
  82.1 3.7 copy-start.5
  87.5 108.9 %all-reduce.22.cloned.1.call-start = ((), (), s32[]{:S(2)}) async-start(), calls=%async_computation.7 | async-start | bytes 4718592 | tf_op jit(solution)/shard_map/psum | solution.py:201
  99.6 142.9 %all-reduce.14.cloned.1.call-start = ((), (), s32[]{:S(2)}) async-start(), calls=%async_computation.3 | async-start | bytes 1572864 | tf_op jit(solution)/shard_map/psum | solution.py:197
  130.7 3.0 copy-start.13
  137.1 2.1 copy-start.66
  137.2 3.0 copy-start.22
  147.4 3.9 copy-start.40
  149.0 2.5 copy-start.74
  149.0 3.2 copy-start.73
  149.1 4.1 copy-start.10
  149.1 4.1 copy-start.39
  149.1 154.0 %all-reduce.20.cloned.1.call-start = ((), (), s32[]{:S(2)}) async-start(), calls=%async_computation.6 | async-start | bytes 2359296 | tf_op jit(solution)/shard_map/psum | solution.py:247
  154.2 42.3 %copy-start.8 = (f32[3,192,768]{2,1,0:T(8,128)S(1)}, f32[3,192,768]{2,1,0:T(8,128)}, u32[]{:S(2)}) copy-start(f32[3,192,768]{2,1,0:T(8,128)} %param.25) | copy-start | bytes 5308420
  196.4 152.2 %all-reduce.16.cloned.1.call-start = ((), (), s32[]{:S(2)}) async-start(), calls=%async_computation.4 | async-start | bytes 1572864 | tf_op jit(solution)/shard_map/psum | solution.py:235
  196.5 2.9 copy-start.6
  199.4 43.5 %copy-start.29 = (bf16[768,768]{1,0:T(8,128)(2,1)S(1)}, bf16[768,768]{1,0:T(8,128)(2,1)}, u32[]{:S(2)}) copy-start(bf16[768,768]{1,0:T(8,128)(2,1)} %get-tuple-element.137) | copy-start | bytes 3538948
  242.5 239.9 %all-reduce.18.cloned.1.call-start = ((), (), s32[]{:S(2)}) async-start(), calls=%async_computation.5 | async-start | bytes 3145728 | tf_op jit(solution)/shard_map/psum | solution.py:299
  246.7 58.5 %copy-start.11 = (f32[3,192,768]{2,1,0:T(8,128)S(1)}, f32[3,192,768]{2,1,0:T(8,128)}, u32[]{:S(2)}) copy-start(f32[3,192,768]{2,1,0:T(8,128)} %broadcast_multiply_fusion.3) | copy-start | bytes 5308420
  305.2 43.4 %copy-start.48 = (f32[2,768]{1,0:T(2,128)S(1)}, f32[2,768]{1,0:T(2,128)}, u32[]{:S(2)}) copy-start(f32[2,768]{1,0:T(2,128)} %copy-done.47) | copy-start | bytes 18436
  305.2 43.4 %copy-start.51 = (f32[2,256]{1,0:T(2,128)S(1)}, f32[2,256]{1,0:T(2,128)}, u32[]{:S(2)}) copy-start(f32[2,256]{1,0:T(2,128)} %copy-done.50) | copy-start | bytes 6148
  305.2 45.1 %copy-start.65 = (f32[2,256]{1,0:T(2,128)S(1)}, f32[2,256]{1,0:T(2,128)}, u32[]{:S(2)}) copy-start(f32[2,256]{1,0:T(2,128)} %copy-done.64) | copy-start | bytes 6148
  308.1 42.3 %copy-start.56 = (f32[2,256]{1,0:T(2,128)S(1)}, f32[2,256]{1,0:T(2,128)}, u32[]{:S(2)}) copy-start(f32[2,256]{1,0:T(2,128)} %copy-done.55) | copy-start | bytes 6148
  308.1 44.3 %copy-start.2 = (f32[2,256,768]{2,1,0:T(8,128)S(1)}, f32[2,256,768]{2,1,0:T(8,128)}, u32[]{:S(2)}) copy-start(f32[2,256,768]{2,1,0:T(8,128)} %add_add_fusion.1) | copy-start | bytes 4718596
  308.1 44.3 %copy-start.46 = (f32[768]{0:T(1024)S(1)}, f32[768]{0:T(1024)}, u32[]{:S(2)}) copy-start(f32[768]{0:T(1024)} %get-tuple-element.198) | copy-start | bytes 9220
  308.1 44.3 %copy-start.54 = (f32[2,768]{1,0:T(2,128)S(1)}, f32[2,768]{1,0:T(2,128)}, u32[]{:S(2)}) copy-start(f32[2,768]{1,0:T(2,128)} %copy-done.53) | copy-start | bytes 18436
  308.1 44.3 %copy-start.67 = (f32[2,256]{1,0:T(2,128)S(1)}, f32[2,256]{1,0:T(2,128)}, u32[]{:S(2)}) copy-start(f32[2,256]{1,0:T(2,128)} %copy-done.66) | copy-start | bytes 6148
  308.1 44.3 %copy-start.68 = (f32[768]{0:T(1024)S(1)}, f32[768]{0:T(1024)}, u32[]{:S(2)}) copy-start(f32[768]{0:T(1024)} %get-tuple-element.197) | copy-start | bytes 9220
  348.6 3.9 copy-start.12
  348.6 3.9 copy-start.15
  352.5 3.8 copy-start.62
  352.5 3.8 copy-start.61
  352.5 3.9 copy-start.3
  356.5 20.4 %copy-start.72 = (bf16[2,768]{1,0:T(2,128)(2,1)S(1)}, bf16[2,768]{1,0:T(2,128)(2,1)}, u32[]{:S(2)}) copy-start(bf16[2,768]{1,0:T(2,128)(2,1)} %param.22) | copy-start | bytes 9220
  366.5 20.0 %copy-start.31 = (f32[8,20,192]{2,1,0:T(8,128)}, f32[8,20,192]{2,1,0:T(8,128)S(1)}, u32[]{:S(2)}) copy-start(f32[8,20,192]{2,1,0:T(8,128)S(1)} %all-gather.2) | copy-start | bytes 368644
  386.5 4.6 copy-start.16
  386.5 4.6 copy-start.18
  408.3 5.1 copy-start.33
  408.3 5.8 copy-start.34
  497.6 4.2 copy-start.19
  497.6 4.2 copy-start.24
  497.6 4.2 copy-start.32
  497.7 4.2 copy-start.36
  497.7 4.2 copy-start.37
  497.7 4.2 copy-start.38
  535.4 21.1 %all-to-all-start = ((bf16[8,768,96]{1,2,0:T(8,128)(2,1)}), bf16[8,768,96]{1,2,0:T(8,128)(2,1)}, u32[]{:S(2)}, u32[]{:S(2)}) async-start(bf16[8,768,96]{1,2,0:T(8,128)(2,1)} %bitcast.262), calls=%async_computation | async-start | bytes 2359296 | tf_op jit(solution)/shard_map/all_to_all | solution.py:304
  546.1 8.6 %copy-start.52 = (f32[14,192]{1,0:T(8,128)S(1)}, f32[14,192]{1,0:T(8,128)}, u32[]{:S(2)}) copy-start(f32[14,192]{1,0:T(8,128)} %param.29) | copy-start | bytes 32260
  546.1 8.6 %copy-start.69 = (f32[14,192]{1,0:T(8,128)S(1)}, f32[14,192]{1,0:T(8,128)}, u32[]{:S(2)}) copy-start(f32[14,192]{1,0:T(8,128)} %param.35) | copy-start | bytes 32260
  546.1 8.6 %copy-start.70 = (f32[14,192]{1,0:T(8,128)S(1)}, f32[14,192]{1,0:T(8,128)}, u32[]{:S(2)}) copy-start(f32[14,192]{1,0:T(8,128)} %param.36) | copy-start | bytes 32260
  (22 other events, 23.5 us)
Sparse Core Ops, SparseCore 0:
  33.8 44.7 all-reduce.9
  87.7 42.9 all-reduce.11
  134.0 62.3 all-reduce.21
  199.3 43.0 all-reduce.13
  246.4 56.6 all-reduce.19
  305.9 42.7 all-reduce.15
  415.0 67.3 all-reduce.17
